TPU v7x, 256 devices: a whole 4x4x8 slice. The times are simulated.
256 devices in a mesh: pts: 128 (over x, z, y), rep: 2 (over core).
Axes of the slice: x: 4, y: 4, z: 8, core: 2. Of those that a mesh axis runs over, the one named last changes fastest.
Arguments:
- feats: bfloat16 [2, 98304, 256], P('rep', 'pts'), may hold values from -6 to 6
- cotangent: bfloat16 [2, 98304, 256], P('rep', 'pts'), may hold values from -6 to 6
- dest: int32 [2, 98304], P('rep', 'pts'), may hold values from 0 to 131071, as said below
- pads: int32 [2, 128], P('rep', 'pts'), may hold values from 0 to 512, as said below
- w_qkv: bfloat16 [256, 768], replicated, may hold values from -24 to 24
- w_out: bfloat16 [256, 256], replicated, may hold values from -0.375 to 0.375
Outputs:
- result: bfloat16 [2, 98304, 256], P('rep', 'pts')
- grad_feats: bfloat16 [2, 98304, 256], P('rep', 'pts')
- grad_qkv: float32 [256, 768], replicated
- grad_out: float32 [256, 256], replicated
Inputs may be any that keep to these rules, and one draw needn't show every extreme that they name: `dest`: each row's slot lies among the 1024 slots of one index of pts; every used slot is named exactly once; at most 10 points go from one index of pts to any one other index of pts, and in every draw some pair of indices reaches exactly 10. `pads`: the used slots of each scan number 98304.
All inputs are finite; a program needn't handle non-finite values.
Results may differ from a plain program's by a relative error of at most 0.015.
The roundings to bfloat16 on the way count: a program that leaves them out, or rounds other values in their place, can miss the bound.
Values may be sent and summed in bfloat16 or wider, within the bound.
A program may use at most 320 MiB of HBM per device.

v0:
```python
import jax
import jax.numpy as jnp
from jax import lax
from jax.sharding import PartitionSpec as P

HEADS = 16
PATCH = 1024
PPD = 1


def normalize(values):
    center = jnp.mean(values, axis=-1, keepdims=True)
    spread = jnp.mean(jnp.square(values - center), axis=-1, keepdims=True)
    return (values - center) * lax.rsqrt(spread + 1e-05)


def attend(qkv, keymask):
    count = qkv.shape[0]
    width = qkv.shape[1] // 3
    channels = width // HEADS
    parts = qkv.reshape(count, 3, HEADS, channels).transpose(1, 2, 0, 3)

    def one_head(item):
        query, keys, values = item
        scores = jnp.dot(query, keys.T, preferred_element_type=jnp.float32) * channels ** (-0.5)
        scores = jnp.where(keymask[None, :], scores, -1e30)
        largest = jnp.max(scores, axis=-1, keepdims=True)
        expo = jnp.exp(scores - largest)
        weights = (expo / jnp.sum(expo, axis=-1, keepdims=True)).astype(jnp.bfloat16)
        return jnp.dot(weights, values, preferred_element_type=jnp.float32).astype(jnp.bfloat16)

    mixed = lax.map(one_head, (parts[0], parts[1], parts[2]))
    return mixed.transpose(1, 0, 2).reshape(count, width)


def forward(slot_rows, keymask, w_qkv, w_out):
    normed = normalize(slot_rows.astype(jnp.float32)).astype(jnp.bfloat16)
    qkv = jnp.dot(normed, w_qkv, preferred_element_type=jnp.float32).astype(jnp.bfloat16)
    attended = attend(qkv, keymask)
    out_rows = (
        slot_rows.astype(jnp.float32) + jnp.dot(attended, w_out, preferred_element_type=jnp.float32)
    ).astype(jnp.bfloat16)
    return (out_rows, normed, qkv, attended)


def backward(cot_rows, slot_rows, normed, qkv, keymask, w_qkv, w_out):
    d_attended = jnp.dot(cot_rows, w_out.T, preferred_element_type=jnp.float32).astype(jnp.bfloat16)
    _, attend_back = jax.vjp(lambda packed: attend(packed, keymask), qkv)
    d_qkv = attend_back(d_attended)[0]
    grad_part = jnp.dot(normed.T, d_qkv, preferred_element_type=jnp.float32)
    d_normed = jnp.dot(d_qkv, w_qkv.T, preferred_element_type=jnp.float32)
    _, norm_back = jax.vjp(normalize, slot_rows.astype(jnp.float32))
    d_rows = (cot_rows.astype(jnp.float32) + norm_back(d_normed)[0]).astype(jnp.bfloat16)
    return (d_rows, grad_part)


def run_forward(slot_feats, masks, w_qkv, w_out):
    width = slot_feats.shape[-1]
    patched = slot_feats.reshape(PPD, PATCH, width)
    return lax.map(lambda item: forward(item[0], item[1], w_qkv, w_out), (patched, masks))


def run_backward(slot_cot, slot_feats, stash, masks, w_qkv, w_out, factor):
    width = slot_cot.shape[-1]
    out_rows, normed, qkv, attended = stash
    grad_out = jnp.dot(attended.reshape(-1, width).T, slot_cot, preferred_element_type=jnp.float32)
    patched_cot = slot_cot.reshape(PPD, PATCH, width)
    patched = slot_feats.reshape(PPD, PATCH, width)
    d_rows, grad_parts = lax.map(
        lambda item: backward(item[0], item[1], item[2], item[3], item[4], w_qkv, w_out),
        (patched_cot, patched, normed, qkv, masks),
    )
    grad_qkv = jnp.sum(grad_parts, axis=0)
    grad_qkv, grad_out = lax.psum((grad_qkv, grad_out), ("pts", "rep"))
    return (d_rows.reshape(-1, width), grad_qkv * factor, grad_out * factor)


def on_device(feats, cotangent, dest, pads, w_qkv, w_out):
    groups = lax.axis_size("pts")
    rows = feats.shape[1]
    width = feats.shape[2]
    slot_dev = PPD * PATCH
    mean_peer = rows // groups
    third = mean_peer // 3
    base = mean_peer - third
    capacity = base + base // 2 + 2 * third
    factor = (groups * lax.axis_size("rep") * rows) ** (-0.5)
    target = dest[0]
    owner = target // slot_dev
    local_slot = target % slot_dev
    onehot = (owner[:, None] == jnp.arange(groups)[None, :]).astype(jnp.int32)
    rank = jnp.sum((jnp.cumsum(onehot, axis=0) - 1) * onehot, axis=1)
    place = owner * capacity + rank

    def pack(values):
        return jnp.zeros((groups * capacity, width), values.dtype).at[place].set(values)

    def spread(received, slots):
        return jnp.zeros((slot_dev, width), jnp.bfloat16).at[slots].set(received, mode="drop")

    slot_buffer = jnp.full((groups * capacity,), slot_dev, jnp.int32).at[place].set(local_slot)
    counts = PATCH - pads[0]
    masks = jnp.arange(PATCH)[None, :] < counts[:, None]
    got_feats, got_slots = (
        lax.all_to_all(pack(feats[0]), "pts", split_axis=0, concat_axis=0, tiled=True),
        lax.all_to_all(slot_buffer, "pts", split_axis=0, concat_axis=0, tiled=True),
    )
    slot_feats = spread(got_feats, got_slots)
    stash = run_forward(slot_feats, masks, w_qkv, w_out)
    pick = jnp.minimum(got_slots, slot_dev - 1)
    out_slots = stash[0].reshape(-1, width)
    back_out = lax.all_to_all(out_slots[pick], "pts", split_axis=0, concat_axis=0, tiled=True)
    got_cot = lax.all_to_all(pack(cotangent[0]), "pts", split_axis=0, concat_axis=0, tiled=True)
    slot_cot = spread(got_cot, got_slots)
    d_slots, grad_qkv, grad_out = run_backward(
        slot_cot, slot_feats, stash, masks, w_qkv, w_out, factor
    )
    back_grad = lax.all_to_all(d_slots[pick], "pts", split_axis=0, concat_axis=0, tiled=True)
    return (back_out[place][None], back_grad[place][None], grad_qkv, grad_out)


def solution(mesh):
    placed = (
        P("rep", "pts", None),
        P("rep", "pts", None),
        P("rep", "pts"),
        P("rep", "pts"),
        P(),
        P(),
    )
    return jax.shard_map(
        on_device,
        mesh=mesh,
        in_specs=placed,
        out_specs=(P("rep", "pts", None), P("rep", "pts", None), P(), P()),
        check_vma=False,
    )
```

profile of v0, /device:TPU:1, one launch (start us, length us, event | category | flops | bytes accessed | tf_op | source)
XLA Modules:
  0.0 963.7 jit_solution(16096121416201060404)
XLA Ops:
  13.7 16.3 %all-to-all-start = ((s32[128,10,1]{1,2,0:T(1,128)}), s32[128,10,1]{1,2,0:T(1,128)S(1)}, u32[]{:S(2)}, u32[]{:S(2)}) async-start(s32[128,10,1]{1,2,0:T(1,128)} %bitcast.4), calls=%async_computation | async-start | bytes 131072 | tf_op jit(solution)/shard_map/all_to_all | solution.py:106
  30.0 6.0 scatter_custom_fusion.1
  40.5 9.9 %all-to-all-start.1 = ((bf16[128,10,256]{2,1,0:T(8,128)(2,1)}), bf16[128,10,256]{2,1,0:T(8,128)(2,1)S(1)}, u32[]{:S(2)}, u32[]{:S(2)}) async-start(bf16[128,10,256]{2,1,0:T(8,128)(2,1)} %all_to_all.43), calls=%async_computation.1 | async-start | bytes 2097152 | tf_op jit(solution)/shard_map/all_to_all | solution.py:105
  51.2 5.9 scatter_custom_fusion.3
  59.9 17.4 %all-to-all-done.1 = bf16[128,10,256]{2,1,0:T(8,128)(2,1)S(1)} async-done(((bf16[128,10,256]{2,1,0:T(8,128)(2,1)}), bf16[128,10,256]{2,1,0:T(8,128)(2,1)S(1)}, u32[]{:S(2)}, u32[]{:S(2)}) %all-to-all-start.1) | async-done | bytes 655392 | tf_op jit(solution)/shard_map/all_to_all | solution.py:105
  77.2 9.1 all-to-all-start.3
  87.4 8.3 scatter_custom_fusion.2
  98.2 201.4 %while.84 = (s32[]{:T(128)}, bf16[16,16,1024]{2,1,0:T(8,128)(2,1)}, f32[16,1024,1024]{1,2,0:T(8,128)}, f32[16,1024]{1,0:T(8,128)}, f32[16,1024,1024]{1,2,0:T(8,1...) while((s32[]{:T(128)}, bf16[16,16,1024]{2,1,0:T(8,128)(2,1)}, ...), condition=%wide.region_18.19_spmd.clone, body=%wide.region_14.18_spmd.clone.sunk | while | flops 53476352 | bytes 29547648 | solution.py:32
  101.4 4.4 fusion.149
  114.0 4.4 fusion.149
  126.6 4.5 fusion.149
  139.2 4.4 fusion.149
  151.8 4.4 fusion.149
  164.3 4.4 fusion.149
  176.9 4.5 fusion.149
  189.6 4.4 fusion.149
  202.1 4.5 fusion.149
  214.8 4.4 fusion.149
  227.4 4.4 fusion.149
  240.0 4.4 fusion.149
  252.5 4.5 fusion.149
  265.2 4.4 fusion.149
  277.7 4.4 fusion.149
  290.3 4.4 fusion.149
  300.7 8.5 scatter_custom_fusion.4
  310.6 253.7 %while.85 = (s32[]{:T(128)}, bf16[16,1024,16]{1,2,0:T(8,128)(2,1)S(1)}, bf16[16,1024,16]{1,2,0:T(8,128)(2,1)S(1)}, bf16[16,1024,16]{1,2,0:T(8,128)(2,1)S(1)}, bf...) while((s32[]{:T(128)}, ...), condition=%wide.region_22.23_spmd.clone, body=%wide.region_19.22_spmd.clone.sunk | while | flops 154158080 | bytes 31803576 | solution.py:32
  397.3 4.3 fusion.158
  573.0 13.5 %all-to-all-start.4 = ((bf16[128,10,256]{2,1,0:T(8,128)(2,1)}), bf16[128,10,256]{2,1,0:T(8,128)(2,1)S(1)}, u32[]{:S(2)}, u32[]{:S(2)}) async-start(bf16[128,10,256]{2,1,0:T(8,128)(2,1)} %all_to_all.52), calls=%async_computation.4 | async-start | bytes 2097152 | tf_op jit(solution)/shard_map/all_to_all | solution.py:118
  586.6 70.5 %while.83 = (s32[]{:T(128)}, bf16[16,1024,16]{1,2,0:T(8,128)(2,1)S(1)}, bf16[16,1024,16]{1,2,0:T(8,128)(2,1)S(1)}, bf16[16,1024,16]{1,2,0:T(8,128)(2,1)}, bf16[1...) while((s32[]{:T(128)}, bf16[16,1024,16]{1,2,0:T(8,128)(2,1)S(1)}, ...), condition=%wide.region_11.12_spmd.clone, body=%wide.region_8.11_spmd.clone.sunk | while | flops 79707136 | bytes 12740689 | solution.py:32
  658.3 4.7 gather_fusion
  665.1 13.9 %all-to-all-start.2 = ((bf16[128,10,256]{2,1,0:T(8,128)(2,1)}), bf16[128,10,256]{2,1,0:T(8,128)(2,1)}, u32[]{:S(2)}, u32[]{:S(2)}) async-start(bf16[128,10,256]{2,1,0:T(8,128)(2,1)} %all_to_all.46), calls=%async_computation.2 | async-start | bytes 2097152 | tf_op jit(solution)/shard_map/all_to_all | solution.py:112
  683.3 261.2 %all-reduce.6.cloned.1.call-done = (f32[256,768]{1,0:T(8,128)}, f32[256,256]{1,0:T(8,128)}) async-done(((f32[256,768]{1,0:T(8,128)}, f32[256,256]{1,0:T(8,128)}), (f32[256,768]{1,0:T(8,128)}, f32[256,256]{1,0:T(8,128)})) %all-reduce.6.cloned.1.call-update) | async-done | bytes 1048592 | tf_op jit(solution)/shard_map/psum | solution.py:74
  (411 shorter events, 497.0 us)
Async XLA Ops:
  7.2 89.1 %copy-start = (bf16[256,768]{1,0:T(8,128)(2,1)S(1)}, bf16[256,768]{1,0:T(8,128)(2,1)}, u32[]{:S(2)}) copy-start(bf16[256,768]{1,0:T(8,128)(2,1)} %param.16) | copy-start | bytes 1179652
  7.2 44.0 %copy-start.4 = (bf16[1,768,256]{2,1,0:T(8,128)(2,1)S(1)}, bf16[1,768,256]{2,1,0:T(8,128)(2,1)}, u32[]{:S(2)}) copy-start(bf16[1,768,256]{2,1,0:T(8,128)(2,1)} %param.13) | copy-start | bytes 1179652
  9.5 67.7 %copy-start.10 = (s32[768]{0:T(1024)}, s32[768]{0:T(1024)S(1)}, u32[]{:S(2)}) copy-start(s32[768]{0:T(1024)S(1)} %fusion.107) | copy-start | bytes 9220
  13.7 26.8 %all-to-all-start = ((s32[128,10,1]{1,2,0:T(1,128)}), s32[128,10,1]{1,2,0:T(1,128)S(1)}, u32[]{:S(2)}, u32[]{:S(2)}) async-start(s32[128,10,1]{1,2,0:T(1,128)} %bitcast.4), calls=%async_computation | async-start | bytes 131072 | tf_op jit(solution)/shard_map/all_to_all | solution.py:106
  40.5 36.7 %all-to-all-start.1 = ((bf16[128,10,256]{2,1,0:T(8,128)(2,1)}), bf16[128,10,256]{2,1,0:T(8,128)(2,1)S(1)}, u32[]{:S(2)}, u32[]{:S(2)}) async-start(bf16[128,10,256]{2,1,0:T(8,128)(2,1)} %all_to_all.43), calls=%async_computation.1 | async-start | bytes 2097152 | tf_op jit(solution)/shard_map/all_to_all | solution.py:105
  59.8 37.4 %copy-start.12 = (s32[1280]{0:T(1024)}, s32[1280]{0:T(1024)S(1)}, u32[]{:S(2)}) copy-start(s32[1280]{0:T(1024)S(1)} %get-tuple-element.621) | copy-start | bytes 15364
  77.2 222.4 %all-to-all-start.3 = ((bf16[128,10,256]{2,1,0:T(8,128)(2,1)}), bf16[128,10,256]{2,1,0:T(8,128)(2,1)S(1)}, u32[]{:S(2)}, u32[]{:S(2)}) async-start(bf16[128,10,256]{2,1,0:T(8,128)(2,1)} %all_to_all.49), calls=%async_computation.3 | async-start | bytes 2097152 | tf_op jit(solution)/shard_map/all_to_all | solution.py:113
  96.3 1.0 copy-start.8
  96.3 0.9 copy-start.5
  98.2 211.0 %copy-start.3 = (bf16[256,256]{1,0:T(8,128)(2,1)S(1)}, bf16[256,256]{1,0:T(8,128)(2,1)}, u32[]{:S(2)}) copy-start(bf16[256,256]{1,0:T(8,128)(2,1)} %param.17) | copy-start | bytes 393220
  299.7 10.7 %copy-start.1 = (bf16[16,1024,16]{1,2,0:T(8,128)(2,1)}, bf16[16,1024,16]{1,2,0:T(8,128)(2,1)S(1)}, u32[]{:S(2)}) copy-start(bf16[16,1024,16]{1,2,0:T(8,128)(2,1)S(1)} %get-tuple-element.1056) | copy-start | bytes 1572868
  564.2 2.0 copy-start.9
  564.2 2.6 copy-start.6
  564.4 2.4 copy-start.2
  573.0 92.1 %all-to-all-start.4 = ((bf16[128,10,256]{2,1,0:T(8,128)(2,1)}), bf16[128,10,256]{2,1,0:T(8,128)(2,1)S(1)}, u32[]{:S(2)}, u32[]{:S(2)}) async-start(bf16[128,10,256]{2,1,0:T(8,128)(2,1)} %all_to_all.52), calls=%async_computation.4 | async-start | bytes 2097152 | tf_op jit(solution)/shard_map/all_to_all | solution.py:118
  658.3 20.8 %copy-start.7 = (f32[1024]{0:T(1024)S(1)}, f32[1024]{0:T(1024)}, u32[]{:S(2)}) copy-start(f32[1024]{0:T(1024)} %copy-done.5) | copy-start | bytes 12292
  665.1 18.2 %copy-start.11 = (s32[768]{0:T(1024)S(1)}, s32[768]{0:T(1024)}, u32[]{:S(2)}) copy-start(s32[768]{0:T(1024)} %copy-done.10) | copy-start | bytes 9220
  665.1 286.7 %all-to-all-start.2 = ((bf16[128,10,256]{2,1,0:T(8,128)(2,1)}), bf16[128,10,256]{2,1,0:T(8,128)(2,1)}, u32[]{:S(2)}, u32[]{:S(2)}) async-start(bf16[128,10,256]{2,1,0:T(8,128)(2,1)} %all_to_all.46), calls=%async_computation.2 | async-start | bytes 2097152 | tf_op jit(solution)/shard_map/all_to_all | solution.py:112
  679.0 265.5 %all-reduce.6.cloned.1.call-start = ((), (), s32[]{:S(2)}) async-start(), calls=%async_computation.5 | async-start | bytes 2097152 | tf_op jit(solution)/shard_map/psum | solution.py:74
Sparse Core Ops, SparseCore 0:
  686.0 258.4 all-reduce.5
where the time goes:
time: 981 us; the launch traced here: 964 us
  other arithmetic  297 us (30%)
  waiting for transfers between devices  282 us (29%)
  matrix products  191 us (19%)
  local copies, waits for them, and re-layouts  115 us (12%)
  starting transfers between devices  62.8 us (6%)
  between operations  15.6 us (2%)
    psum x1, waiting for transfers between devices, run_backward(): grad_qkv, grad_out = lax.psum((grad_qkv, grad_out), ('pts', 'rep'))  261 us
    dynamic_update_slice x48, other arithmetic, attend(): mixed = lax.map(one_head, (parts[0], parts[1], parts[2]))  119 us
    dot_general x48, matrix products, one_head(): jnp.dot(weights, values, preferred_element_type=jnp.float32)  115 us
    mul x16, other arithmetic, one_head(): jnp.dot(query, keys.T, preferred_element_type=jnp.float32)  69 us
    dot_general x64, matrix products, one_head(): jnp.dot(query, keys.T, preferred_element_type=jnp.float32)  66.3 us
    reduce_sum x16, other arithmetic, one_head(): expo = jnp.exp(scores - largest)  47.4 us
    reduce_sum x16, other arithmetic, one_head(): largest = jnp.max(scores, axis=-1, keepdims=True)  37.6 us
    dynamic_update_slice x32, local copies, waits for them, and re-layouts, attend(): mixed = lax.map(one_head, (parts[0], parts[1], parts[2]))  31.9 us
  transfers between devices with their start and end apart: 6, of which 3 were waited for; matrix products, arithmetic and copies ran while one was open for 33% of the time, Pallas kernels for 0%

commit v1 on v0

v1 whole, which is shorter than its diff:
```python
import functools

import jax
import jax.numpy as jnp
from jax import lax
from jax.experimental import pallas as pl
from jax.experimental.pallas import tpu as pltpu
from jax.sharding import PartitionSpec as P

HEADS = 16
CH = 16
PATCH = 1024
CAP = 10
CHUNK = 24
BF = jnp.bfloat16
F32 = jnp.float32


def dg(a, b, ca, cb):
    return lax.dot_general(a, b, (((ca,), (cb,)), ((), ())), preferred_element_type=F32)


def iota(shape, dim):
    return lax.broadcasted_iota(jnp.int32, shape, dim)


def kernel(
    n, factor,
    feats, cot, dest, pads, w_qkv, w_out,
    out_r, out_g, out_wq, out_wo,
    pick, back, seat, stage, send_a, send_b, got_f, got_c, got_r, got_g,
    rows, x32, c16, norm, qkv, d_qkv, att, d_att, o32, inv, expo, d_s,
    grads, parts, total, other, whole,
    send_sem, recv_sem, pair_sem,
):
    me = lax.axis_index("pts")
    rep = lax.axis_index("rep")
    width = feats.shape[1]
    points = feats.shape[0]

    barrier = pltpu.get_barrier_semaphore()

    def greet(j, _):
        pl.semaphore_signal(
            barrier, inc=1, device_id=(lax.rem(me + j, n), rep), device_id_type=pl.DeviceIdType.MESH
        )
        return 0

    lax.fori_loop(1, n, greet, 0)
    pl.semaphore_signal(barrier, inc=1, device_id=(me, 1 - rep), device_id_type=pl.DeviceIdType.MESH)

    def chunk_copy(src, dst, which, peer):
        return pltpu.make_async_remote_copy(
            src_ref=src.at[peer],
            dst_ref=dst.at[me],
            send_sem=send_sem.at[which],
            recv_sem=recv_sem.at[which],
            device_id=(peer, rep),
            device_id_type=pl.DeviceIdType.MESH,
        )

    def send_some(src, dst, which, lo, hi):
        def one(j, _):
            chunk_copy(src, dst, which, lax.rem(me + j, n)).start()
            return 0

        lax.fori_loop(lo, hi, one, 0)

    def send_own(src, dst, which):
        pltpu.make_async_copy(src.at[me], dst.at[me], recv_sem.at[which]).start()

    def wait_got(dst, which):
        pltpu.make_async_copy(dst, dst, recv_sem.at[which]).wait()

    def wait_sent(src, which):
        part = src.at[pl.ds(0, n - 1)]
        pltpu.make_async_copy(part, part, send_sem.at[which]).wait()

    def to_chunks(values, dst):
        for k in range(CAP):
            for c in range(2):
                stage[pl.ds(c * CAP + k, n, stride=CHUNK), :] = values[
                    k * n : (k + 1) * n, c * 128 : (c + 1) * 128
                ]
        dst[...] = stage[...].reshape(n, CHUNK, 128).astype(BF)

    def from_chunks(src):
        stage[...] = src[...].astype(F32).reshape(n * CHUNK, 128)
        for k in range(CAP):
            for c in range(2):
                rows[k * n : (k + 1) * n, c * 128 : (c + 1) * 128] = stage[
                    pl.ds(c * CAP + k, n, stride=CHUNK), :
                ].astype(BF)

    target = dest[...]
    owner = lax.shift_right_logical(target, 10)
    code = (target & (PATCH - 1)) + 1
    owner_hot = (iota((n, points), 0) == owner).astype(F32).astype(BF)
    upper = (iota((points, points), 0) < iota((points, points), 1)).astype(F32).astype(BF)
    before = jnp.dot(owner_hot, upper, preferred_element_type=F32)
    rank = jnp.sum(before * owner_hot.astype(F32), axis=0, keepdims=True)
    place = rank * float(n) + owner.astype(F32)
    pick[...] = (iota((CAP * n, points), 0) == place.astype(jnp.int32)).astype(F32).astype(BF)
    high = lax.shift_right_logical(code, 5).astype(F32)
    low = (code & 31).astype(F32)
    lane = iota((128, points), 0).astype(F32)
    marks = (jnp.where(lane == rank, high, 0.0) + jnp.where(lane == rank + 16.0, low, 0.0)).astype(BF)
    stage[...] = jnp.zeros(stage.shape, F32)
    stage[pl.ds(2 * CAP, n, stride=CHUNK), :] = dg(owner_hot, marks, 1, 1)
    to_chunks(jnp.dot(pick[...], feats[...], preferred_element_type=F32), send_a)

    pl.semaphore_wait(barrier, n)

    send_some(send_a, got_f, 0, 1, n)
    send_own(send_a, got_f, 0)
    to_chunks(jnp.dot(pick[...], cot[...], preferred_element_type=F32), send_b)
    place_col = jnp.transpose(jnp.broadcast_to(place, (8, points)))[:, :1].astype(jnp.int32)
    back[...] = (iota((points, CAP * n), 1) == place_col).astype(F32).astype(BF)
    wait_got(got_f, 0)
    send_some(send_b, got_c, 1, 1, n)
    send_own(send_b, got_c, 1)

    from_chunks(got_f)
    marked = stage[pl.ds(2 * CAP, n, stride=CHUNK), :]
    for k in range(CAP):
        column = (32.0 * marked[:, k : k + 1] + marked[:, 16 + k : 17 + k]).astype(jnp.int32)
        seat[k * n : (k + 1) * n, :] = (iota((n, PATCH), 1) + 1 == column).astype(F32).astype(BF)
    x32[...] = dg(rows[...], seat[...], 0, 0)

    values = x32[...]
    center = jnp.mean(values, axis=0, keepdims=True)
    spread = jnp.mean(jnp.square(values - center), axis=0, keepdims=True)
    scale = lax.rsqrt(spread + 1e-05)
    norm[...] = ((values - center) * scale).astype(BF)
    qkv[...] = dg(w_qkv[...], norm[...], 0, 0).astype(BF)

    count = PATCH - pads[0, 0]
    first = iota((CH, PATCH), 0) == 0
    bias = jnp.where(first & (iota((CH, PATCH), 1) >= count), -1e30, 0.0).astype(BF)
    ones = jnp.where(iota((CH, PATCH), 0) == 0, 1.0, 0.0).astype(BF)
    pair = jnp.where(iota((CH, PATCH), 0) < 2, 1.0, 0.0).astype(BF)
    q_scale = float(CH ** -0.5 * 1.4426950408889634)
    half = PATCH // 2

    def forward(h, _):
        r = pl.multiple_of(h * CH, CH)
        q = qkv[pl.ds(r, CH), :].astype(F32) * q_scale
        k = qkv[pl.ds(width + r, CH), :]
        v = qkv[pl.ds(2 * width + r, CH), :]
        q_hi = q.astype(BF)
        q_lo = (q - q_hi.astype(F32)).astype(BF)
        left = jnp.concatenate([k, k, bias], axis=0)
        right = jnp.concatenate([q_hi, q_lo, ones], axis=0)
        for j in range(2):
            cols = slice(j * half, (j + 1) * half)
            s = dg(left, right[:, cols], 0, 0)
            m = jnp.max(s, axis=0, keepdims=True)
            e = jnp.exp2(s - m)
            reci = 1.0 / jnp.sum(e, axis=0, keepdims=True)
            e = e.astype(BF)
            expo[h, :, cols] = e
            inv[h, :, cols] = reci
            o32[pl.ds(r, CH), cols] = jnp.dot(v, e, preferred_element_type=F32) * reci
        return 0

    lax.fori_loop(0, HEADS, forward, 0)

    att[...] = o32[...].astype(BF)
    out_t = (x32[...] + dg(w_out[...], att[...], 0, 0)).astype(BF)
    wait_sent(send_a, 0)
    to_chunks(dg(seat[...], out_t, 1, 1), send_a)
    wait_got(got_c, 1)
    send_some(send_a, got_r, 2, 1, n)
    send_own(send_a, got_r, 2)
    from_chunks(got_c)
    c16[...] = dg(rows[...], seat[...], 0, 0).astype(BF)
    d_att[...] = jnp.dot(w_out[...], c16[...], preferred_element_type=F32).astype(BF)
    grads[:, 3 * width :] = dg(att[...], c16[...], 1, 1).astype(BF)

    def backward(h, _):
        r = pl.multiple_of(h * CH, CH)
        q = qkv[pl.ds(r, CH), :]
        k = qkv[pl.ds(width + r, CH), :]
        v = qkv[pl.ds(2 * width + r, CH), :]
        d_o = d_att[pl.ds(r, CH), :].astype(F32)
        reci = inv[h]
        delta = jnp.sum(d_o * o32[pl.ds(r, CH), :], axis=0, keepdims=True) * (-reci)
        d_o = d_o * reci
        d_hi = d_o.astype(BF)
        d_lo = (d_o - d_hi.astype(F32)).astype(BF)
        delta_hi = delta.astype(BF).astype(F32)
        delta_lo = delta - delta_hi
        row = iota((CH, PATCH), 0)
        extra = jnp.where(row == 0, delta_hi, jnp.where(row == 1, delta_lo, 0.0)).astype(BF)
        left = jnp.concatenate([v, v, pair], axis=0)
        right = jnp.concatenate([d_hi, d_lo, extra], axis=0)
        for j in range(2):
            cols = slice(j * half, (j + 1) * half)
            t = dg(left, right[:, cols], 0, 0)
            e = (expo[h, :, cols].astype(F32) * t).astype(BF)
            d_s[:, cols] = e
            d_qkv[pl.ds(r, CH), cols] = (jnp.dot(k, e, preferred_element_type=F32) * 0.25).astype(BF)
        d_qkv[pl.ds(2 * width + r, CH), :] = dg(d_hi, expo[h], 1, 1).astype(BF)
        d_qkv[pl.ds(width + r, CH), :] = (dg(q, d_s[...], 1, 1) * 0.25).astype(BF)
        return 0

    lax.fori_loop(0, HEADS, backward, 0)

    grads[:, : 3 * width] = dg(norm[...], d_qkv[...], 1, 1).astype(BF)

    def block(ref, p):
        return ref.at[
            pl.ds(pl.multiple_of((p // 8) * 16, 16), 16), pl.ds(pl.multiple_of((p % 8) * 128, 128), 128)
        ]

    def spread_part(j, _):
        peer = lax.rem(me + j, n)
        pltpu.make_async_remote_copy(
            src_ref=block(grads, peer),
            dst_ref=parts.at[me],
            send_sem=send_sem.at[4],
            recv_sem=recv_sem.at[4],
            device_id=(peer, rep),
            device_id_type=pl.DeviceIdType.MESH,
        ).start()
        return 0

    lax.fori_loop(1, n, spread_part, 0)
    pltpu.make_async_copy(block(grads, me), parts.at[me], recv_sem.at[4]).start()

    d_norm = jnp.dot(w_qkv[...], d_qkv[...], preferred_element_type=F32)
    values = x32[...]
    center = jnp.mean(values, axis=0, keepdims=True)
    spread = jnp.mean(jnp.square(values - center), axis=0, keepdims=True)
    scale = lax.rsqrt(spread + 1e-05)
    unit = (values - center) * scale
    along = jnp.mean(d_norm * unit, axis=0, keepdims=True)
    level = jnp.mean(d_norm, axis=0, keepdims=True)
    d_rows = (c16[...].astype(F32) + scale * (d_norm - level - unit * along)).astype(BF)
    wait_sent(send_b, 1)
    to_chunks(dg(seat[...], d_rows, 1, 1), send_b)
    send_some(send_b, got_g, 3, 1, n)
    send_own(send_b, got_g, 3)

    wait_got(parts, 4)
    total[...] = jnp.sum(parts[...].astype(F32), axis=0)
    swap = pltpu.make_async_remote_copy(
        src_ref=total, dst_ref=other, send_sem=pair_sem.at[0], recv_sem=pair_sem.at[1],
        device_id=(me, 1 - rep), device_id_type=pl.DeviceIdType.MESH,
    )
    swap.start()
    swap.wait()
    mine = ((total[...] + other[...]) * factor).astype(BF)
    parts[0] = mine

    def share(j, _):
        peer = lax.rem(me + j, n)
        pltpu.make_async_remote_copy(
            src_ref=parts.at[0],
            dst_ref=block(whole, me),
            send_sem=send_sem.at[5],
            recv_sem=recv_sem.at[5],
            device_id=(peer, rep),
            device_id_type=pl.DeviceIdType.MESH,
        ).start()
        return 0

    lax.fori_loop(1, n, share, 0)
    pltpu.make_async_copy(parts.at[0], block(whole, me), recv_sem.at[5]).start()

    wait_got(got_r, 2)
    from_chunks(got_r)
    out_r[...] = jnp.dot(back[...], rows[...], preferred_element_type=F32).astype(BF)
    wait_got(got_g, 3)
    from_chunks(got_g)
    out_g[...] = jnp.dot(back[...], rows[...], preferred_element_type=F32).astype(BF)
    pltpu.make_async_copy(whole, whole, recv_sem.at[5]).wait()
    out_wq[...] = whole[:, : 3 * width].astype(F32)
    out_wo[...] = whole[:, 3 * width :].astype(F32)
    wait_sent(send_a, 2)
    wait_sent(send_b, 3)
    wait_sent(parts, 4)
    wait_sent(parts, 5)


def on_device(feats, cotangent, dest, pads, w_qkv, w_out):
    n = lax.axis_size("pts")
    points = feats.shape[1]
    width = feats.shape[2]
    factor = float((n * lax.axis_size("rep") * points) ** (-0.5))
    vmem = pl.BlockSpec(memory_space=pltpu.VMEM)
    got = pl.pallas_call(
        functools.partial(kernel, n, factor),
        out_shape=(
            jax.ShapeDtypeStruct((points, width), BF),
            jax.ShapeDtypeStruct((points, width), BF),
            jax.ShapeDtypeStruct((width, 3 * width), F32),
            jax.ShapeDtypeStruct((width, width), F32),
        ),
        in_specs=[vmem, vmem, vmem, pl.BlockSpec(memory_space=pltpu.SMEM), vmem, vmem],
        out_specs=(vmem, vmem, vmem, vmem),
        scratch_shapes=[
            pltpu.VMEM((CAP * n, points), BF),
            pltpu.VMEM((points, CAP * n), BF),
            pltpu.VMEM((CAP * n, PATCH), BF),
            pltpu.VMEM((n * CHUNK, 128), F32),
            *[pltpu.VMEM((n, CHUNK, 128), BF)] * 6,
            pltpu.VMEM((CAP * n, width), BF),
            pltpu.VMEM((width, PATCH), F32),
            pltpu.VMEM((width, PATCH), BF),
            pltpu.VMEM((width, PATCH), BF),
            pltpu.VMEM((3 * width, PATCH), BF),
            pltpu.VMEM((3 * width, PATCH), BF),
            pltpu.VMEM((width, PATCH), BF),
            pltpu.VMEM((width, PATCH), BF),
            pltpu.VMEM((width, PATCH), F32),
            pltpu.VMEM((HEADS, 1, PATCH), F32),
            pltpu.VMEM((HEADS, PATCH, PATCH), BF),
            pltpu.VMEM((PATCH, PATCH), BF),
            pltpu.VMEM((width, 4 * width), BF),
            pltpu.VMEM((n, 16, 128), BF),
            pltpu.VMEM((16, 128), F32),
            pltpu.VMEM((16, 128), F32),
            pltpu.VMEM((width, 4 * width), BF),
            pltpu.SemaphoreType.DMA((6,)),
            pltpu.SemaphoreType.DMA((6,)),
            pltpu.SemaphoreType.DMA((2,)),
        ],
        compiler_params=pltpu.CompilerParams(
            collective_id=0, has_side_effects=True, vmem_limit_bytes=62 * 2**20
        ),
        cost_estimate=pl.CostEstimate(flops=4 * 10**9, bytes_accessed=4 * 10**6, transcendentals=17 * 10**6),
    )(feats[0], cotangent[0], dest, pads, w_qkv, w_out)
    return (got[0][None], got[1][None], got[2], got[3])


def solution(mesh):
    placed = (
        P("rep", "pts", None),
        P("rep", "pts", None),
        P("rep", "pts"),
        P("rep", "pts"),
        P(),
        P(),
    )
    return jax.shard_map(
        on_device,
        mesh=mesh,
        in_specs=placed,
        out_specs=(P("rep", "pts", None), P("rep", "pts", None), P(), P()),
        check_vma=False,
    )
```

time: 981 us -> 156 us (0.16); the launches traced: 964 us -> 155 us
  other arithmetic: 297 us -> 0 us
  waiting for transfers between devices: 282 us -> 0 us
  matrix products: 191 us -> 0 us
  Pallas kernels: 0 us -> 150 us
  local copies, waits for them, and re-layouts: 115 us -> 4.41 us
  starting transfers between devices: 62.8 us -> 0 us
  between operations: 15.6 us -> 1.31 us
    psum x1 -> x0, waiting for transfers between devices: 261 us -> none  [run_backward(): grad_qkv, grad_out = lax.psum((grad_qkv, grad_out), ('pts', 'rep'))]
    dot_general x118 -> x0, matrix products: 191 us -> none  [the longest x48 115 us: one_head(): jnp.dot(weights, values, preferred_element_type=jnp.float32)]
    pallas_call x0 -> x1, Pallas kernels: none -> 150 us  [on_device(): pl.pallas_call(functools.partial(kernel, n, factor), out_shape=(jax.Shape...]
    dynamic_update_slice x48 -> x0, other arithmetic: 119 us -> none  [attend(): mixed = lax.map(one_head, (parts[0], parts[1], parts[2]))]
    reduce_sum x52 -> x0, other arithmetic: 101 us -> none  [the longest x16 47.4 us: one_head(): expo = jnp.exp(scores - largest)]
    mul x19 -> x0, other arithmetic: 72.7 us -> none  [the longest x16 69 us: one_head(): jnp.dot(query, keys.T, preferred_element_type=jnp.float32)]
    all_to_all x5 -> x0, starting transfers between devices: 62.7 us -> none  [the longest x1 16.3 us: on_device(): lax.all_to_all(slot_buffer, 'pts', split_axis=0, concat_axis=0, tiled=True)]
    scatter x5 -> x0, local copies, waits for them, and re-layouts: 32.1 us -> none  [the longest x2 16.8 us: spread(): jnp.zeros((slot_dev, width), jnp.bfloat16).at[slots]]
  transfers between devices with their start and end apart: 6 -> 0, of which waited for: 3 -> 0; matrix products, arithmetic and copies ran while one was open for 33% -> 0% of each run, Pallas kernels for 0% -> 0%
where the time goes in v1:
time: 156 us; the launch traced here: 155 us
  Pallas kernels  150 us (96%)
  local copies, waits for them, and re-layouts  4.41 us (3%)
    pallas_call x1, Pallas kernels, on_device(): pl.pallas_call(functools.partial(kernel, n, factor), out_shape=(jax.Shape...  150 us
    unnamed x10, local copies, waits for them, and re-layouts  4.41 us

profile of v1, /device:TPU:1, one launch (start us, length us, event | category | flops | bytes accessed | tf_op | source)
XLA Modules:
  0.0 155.4 jit_solution(4524371805612111359)
XLA Ops:
  1.3 149.7 %shard_map.93 = (bf16[768,256]{1,0:T(8,128)(2,1)}, bf16[768,256]{1,0:T(8,128)(2,1)}, f32[256,768]{1,0:T(8,128)}, f32[256,256]{1,0:T(8,128)}) custom-call(bf16[768,256]{1,0:T(8,128)(2,1)} %bitcast.6, bf16[768,256]{1,0:T(8,128)(2,1)} %bitcast.7, s32[1,768]{1,0:T(1,128)} %dest.1, s32[1,1]{1,0:T(1,128)S(6)} %copy.14.pads, bf16[256,768]{1,0:T(8,128)(2,1)} %w_qkv.1, ...), custom_call_target="tpu_custom_call" | custom-call | flops 4000000000 | bytes 4000000 | tf_op jit(solution)/shard_map/pallas_call | solution.py:292
  150.9 0.0 copy-start.1
  151.0 0.0 copy-start
  151.0 1.9 %copy.15 = bf16[1,768,256]{2,1,0:T(8,128)(2,1)} copy(bf16[1,768,256]{2,1,0:T(8,128)(2,1)} %bitcast.5) | data formatting | bytes 786432
  152.8 0.0 copy-done.1
  152.8 0.7 copy.16
  153.6 0.0 copy-done
  153.6 0.0 copy-start.2
  153.6 0.9 copy.17
  154.5 0.2 copy-done.2
  154.7 0.7 copy.18
Async XLA Ops:
  150.9 1.9 %copy-start.1 = (bf16[768,256]{1,0:T(8,128)(2,1)S(1)}, bf16[768,256]{1,0:T(8,128)(2,1)}, u32[]{:S(2)}) copy-start(bf16[768,256]{1,0:T(8,128)(2,1)} %get-tuple-element.9) | copy-start | bytes 1179652
  151.0 2.6 %copy-start = (f32[256,768]{1,0:T(8,128)S(1)}, f32[256,768]{1,0:T(8,128)}, u32[]{:S(2)}) copy-start(f32[256,768]{1,0:T(8,128)} %get-tuple-element.18) | copy-start | bytes 2359300
  153.6 1.1 copy-start.2

commit v2 on v1

v2 whole, which is shorter than its diff:
```python
import functools

import jax
import jax.numpy as jnp
from jax import lax
from jax.experimental import pallas as pl
from jax.experimental.pallas import tpu as pltpu
from jax.sharding import PartitionSpec as P

HEADS = 16
CH = 16
PATCH = 1024
CAP = 10
CHUNK = 24
EARLY = 10
MIX = 45
UNMIX = 37
BF = jnp.bfloat16
F32 = jnp.float32


def dg(a, b, ca, cb):
    return lax.dot_general(a, b, (((ca,), (cb,)), ((), ())), preferred_element_type=F32)


def iota(shape, dim):
    return lax.broadcasted_iota(jnp.int32, shape, dim)


def kernel(
    n, factor,
    feats, cot, dest, pads, w_qkv, w_out,
    out_r, out_g, out_wq, out_wo,
    back, seat, stage, send_a, send_b, got_f, got_c, got_r, got_g,
    rows, x16, c16, norm, qkv, att, d_att, o32, inv, expo,
    grads, parts, total, other, whole,
    send_sem, recv_sem, pair_sem,
):
    me = lax.axis_index("pts")
    rep = lax.axis_index("rep")
    width = feats.shape[1]
    points = feats.shape[0]

    barrier = pltpu.get_barrier_semaphore()

    def greet(j, _):
        pl.semaphore_signal(
            barrier, inc=1, device_id=(lax.rem(me + j, n), rep), device_id_type=pl.DeviceIdType.MESH
        )
        return 0

    lax.fori_loop(1, n, greet, 0)
    pl.semaphore_signal(barrier, inc=1, device_id=(me, 1 - rep), device_id_type=pl.DeviceIdType.MESH)

    def chunk_copy(src, dst, which, peer):
        return pltpu.make_async_remote_copy(
            src_ref=src.at[peer],
            dst_ref=dst.at[me],
            send_sem=send_sem.at[which],
            recv_sem=recv_sem.at[which],
            device_id=(peer, rep),
            device_id_type=pl.DeviceIdType.MESH,
        )

    def send_some(src, dst, which, lo, hi):
        def one(j, _):
            chunk_copy(src, dst, which, lax.rem(me + j, n)).start()
            return 0

        lax.fori_loop(lo, hi, one, 0)

    def send_own(src, dst, which):
        pltpu.make_async_copy(src.at[me], dst.at[me], recv_sem.at[which]).start()

    def wait_got(dst, which):
        pltpu.make_async_copy(dst, dst, recv_sem.at[which]).wait()

    def wait_sent(src, which):
        part = src.at[pl.ds(0, n - 1)]
        pltpu.make_async_copy(part, part, send_sem.at[which]).wait()

    def to_chunks(values, dst):
        for k in range(CAP):
            for c in range(2):
                stage[pl.ds(c * CAP + k, n, stride=CHUNK), :] = values[
                    k * n : (k + 1) * n, c * 128 : (c + 1) * 128
                ]
        dst[...] = stage[...].reshape(n, CHUNK, 128).astype(BF)

    def from_chunks(src):
        stage[...] = src[...].astype(F32).reshape(n * CHUNK, 128)
        for k in range(CAP):
            for c in range(2):
                rows[k * n : (k + 1) * n, c * 128 : (c + 1) * 128] = stage[
                    pl.ds(c * CAP + k, n, stride=CHUNK), :
                ].astype(BF)

    target = dest[...]
    owner = lax.shift_right_logical(target, 10)
    code = (target & (PATCH - 1)) + 1
    owner_hot = (iota((n, points), 0) == owner).astype(F32).astype(BF)
    upper = (iota((points, points), 0) < iota((points, points), 1)).astype(F32).astype(BF)
    before = jnp.dot(owner_hot, upper, preferred_element_type=F32)
    rank = jnp.sum(before * owner_hot.astype(F32), axis=0, keepdims=True)
    place = rank * float(n) + owner.astype(F32)
    pick = (iota((CAP * n, points), 0) == place.astype(jnp.int32)).astype(F32).astype(BF)
    high = lax.shift_right_logical(code, 5).astype(F32)
    low = (code & 31).astype(F32)
    lane = iota((128, points), 0).astype(F32)
    marks = (jnp.where(lane == rank, high, 0.0) + jnp.where(lane == rank + 16.0, low, 0.0)).astype(BF)
    stage[...] = jnp.zeros(stage.shape, F32)
    stage[pl.ds(2 * CAP, n, stride=CHUNK), :] = dg(owner_hot, marks, 1, 1)
    to_chunks(jnp.dot(pick, feats[...], preferred_element_type=F32), send_a)
    to_chunks(jnp.dot(pick, cot[...], preferred_element_type=F32), send_b)

    pl.semaphore_wait(barrier, n)

    send_some(send_a, got_f, 0, 1, n)
    send_own(send_a, got_f, 0)
    place_col = jnp.transpose(jnp.broadcast_to(place, (8, points)))[:, :1].astype(jnp.int32)
    back[...] = (iota((points, CAP * n), 1) == place_col).astype(F32).astype(BF)
    wait_got(got_f, 0)
    send_some(send_b, got_c, 1, 1, 2)
    send_own(send_b, got_c, 1)

    from_chunks(got_f)
    marked = stage[pl.ds(2 * CAP, n, stride=CHUNK), :]
    for k in range(CAP):
        column = (32.0 * marked[:, k : k + 1] + marked[:, 16 + k : 17 + k]).astype(jnp.int32)
        seat[k * n : (k + 1) * n, :] = (iota((n, PATCH), 1) + 1 == column).astype(F32).astype(BF)
    x16[...] = dg(rows[...], seat[...], 0, 0).astype(BF)

    values = x16[...].astype(F32)
    center = jnp.mean(values, axis=0, keepdims=True)
    spread = jnp.mean(jnp.square(values - center), axis=0, keepdims=True)
    scale = lax.rsqrt(spread + 1e-05)
    norm[...] = ((values - center) * scale).astype(BF)
    qkv[...] = dg(w_qkv[...], norm[...], 0, 0).astype(BF)

    count = PATCH - pads[0, 0]
    first = iota((CH, PATCH), 0) == 0
    bias = jnp.where(first & (iota((CH, PATCH), 1) >= count), -1e30, 0.0).astype(BF)
    ones = jnp.where(iota((CH, PATCH), 0) == 0, 1.0, 0.0).astype(BF)
    pair = jnp.where(iota((CH, PATCH), 0) < 2, 1.0, 0.0).astype(BF)
    q_scale = float(CH ** -0.5 * 1.4426950408889634)

    def forward(step, first_peer, sends):
        for i in range(sends):
            chunk_copy(send_b, got_c, 1, lax.rem(me + first_peer + step * sends + i, n)).start()
        pending = None
        for u in range(2):
            h = step * 2 + u
            r = pl.multiple_of(h * CH, CH)
            q = qkv[pl.ds(r, CH), :].astype(F32) * q_scale
            k = qkv[pl.ds(width + r, CH), :]
            v = qkv[pl.ds(2 * width + r, CH), :]
            q_hi = q.astype(BF)
            q_lo = (q - q_hi.astype(F32)).astype(BF)
            left = jnp.concatenate([k, k, bias], axis=0)
            right = jnp.concatenate([q_hi, q_lo, ones], axis=0)
            s = dg(left, right, 0, 0)
            if pending is not None:
                pending()
            m = jnp.max(s, axis=0, keepdims=True)
            e = jnp.exp2(s - m)
            reci = 1.0 / jnp.sum(e, axis=0, keepdims=True)
            e = e.astype(BF)
            expo[h] = e
            inv[h] = reci

            def pending(r=r, v=v, e=e, reci=reci):
                o32[pl.ds(r, CH), :] = jnp.dot(v, e, preferred_element_type=F32) * reci

        pending()

    def forward_sending(step, _):
        forward(step, 2, 21)
        return 0

    def forward_plain(step, _):
        forward(step, 0, 0)
        return 0

    lax.fori_loop(0, 6, forward_sending, 0)
    lax.fori_loop(6, HEADS // 2, forward_plain, 0)

    att[...] = o32[...].astype(BF)
    out_t = (x16[...].astype(F32) + dg(w_out[...], att[...], 0, 0)).astype(BF)
    wait_sent(send_a, 0)
    to_chunks(dg(seat[...], out_t, 1, 1), send_a)
    wait_got(got_c, 1)
    send_some(send_a, got_r, 2, 1, 3)
    send_own(send_a, got_r, 2)
    from_chunks(got_c)
    c16[...] = dg(rows[...], seat[...], 0, 0).astype(BF)
    d_att[...] = jnp.dot(w_out[...], c16[...], preferred_element_type=F32).astype(BF)
    grads[:width, :] = dg(att[...], c16[...], 1, 1).astype(BF)

    def backward(step, first_peer, sends):
        for i in range(sends):
            chunk_copy(send_a, got_r, 2, lax.rem(me + first_peer + step * sends + i, n)).start()
        row = iota((CH, PATCH), 0)
        pending = None
        for u in range(2):
            h = step * 2 + u
            r = pl.multiple_of(h * CH, CH)
            q = qkv[pl.ds(r, CH), :]
            k = qkv[pl.ds(width + r, CH), :]
            v = qkv[pl.ds(2 * width + r, CH), :]
            d_o = d_att[pl.ds(r, CH), :].astype(F32)
            reci = inv[h]
            delta = jnp.sum(d_o * o32[pl.ds(r, CH), :], axis=0, keepdims=True) * (-reci)
            d_o = d_o * reci
            d_hi = d_o.astype(BF)
            d_lo = (d_o - d_hi.astype(F32)).astype(BF)
            delta_hi = delta.astype(BF).astype(F32)
            delta_lo = delta - delta_hi
            extra = jnp.where(row == 0, delta_hi, jnp.where(row == 1, delta_lo, 0.0)).astype(BF)
            left = jnp.concatenate([v, v, pair], axis=0)
            right = jnp.concatenate([d_hi, d_lo, extra], axis=0)
            t = dg(left, right, 0, 0)
            d_v = dg(d_hi, expo[h], 1, 1)
            e = (expo[h].astype(F32) * t).astype(BF)
            if pending is not None:
                pending()
            expo[h] = e
            qkv[pl.ds(2 * width + r, CH), :] = d_v.astype(BF)

            def pending(r=r, k=k, q=q, h=h):
                e = expo[h]
                qkv[pl.ds(r, CH), :] = (jnp.dot(k, e, preferred_element_type=F32) * 0.25).astype(BF)
                qkv[pl.ds(width + r, CH), :] = (dg(q, e, 1, 1) * 0.25).astype(BF)

        pending()

    def backward_sending(step, _):
        backward(step, 3, 25)
        return 0

    def backward_plain(step, _):
        backward(step, 0, 0)
        return 0

    early = EARLY * CH
    late = width - early
    tiles = (width + 3 * early) // 8
    mine = lax.rem(me * UNMIX, n)
    is_early = mine < tiles

    def tile(ref, t):
        return ref.at[
            pl.ds(pl.multiple_of((t // 2) * 16, 16), 16), pl.ds(pl.multiple_of((t % 2) * 128, 128), 128)
        ]

    def send_tiles(lo, hi):
        def one(j, _):
            t = lo + lax.rem(j + me, hi - lo)
            peer = lax.rem(t * MIX, n)

            @pl.when(peer != me)
            def _():
                pltpu.make_async_remote_copy(
                    src_ref=tile(grads, t),
                    dst_ref=parts.at[me],
                    send_sem=send_sem.at[4],
                    recv_sem=recv_sem.at[4],
                    device_id=(peer, rep),
                    device_id_type=pl.DeviceIdType.MESH,
                ).start()

            @pl.when(peer == me)
            def _():
                pltpu.make_async_copy(tile(grads, mine), parts.at[me], recv_sem.at[4]).start()

            return 0

        lax.fori_loop(0, hi - lo, one, 0)

    def swap():
        return pltpu.make_async_remote_copy(
            src_ref=total, dst_ref=other, send_sem=pair_sem.at[0], recv_sem=pair_sem.at[1],
            device_id=(me, 1 - rep), device_id_type=pl.DeviceIdType.MESH,
        )

    def sum_tile():
        wait_got(parts, 4)
        total[...] = jnp.sum(parts[...].astype(F32), axis=0)
        swap().start()

    def share_tile():
        swap().wait()
        parts[0] = ((total[...] + other[...]) * factor).astype(BF)

        def one(j, _):
            pltpu.make_async_remote_copy(
                src_ref=parts.at[0],
                dst_ref=tile(whole, mine),
                send_sem=send_sem.at[5],
                recv_sem=recv_sem.at[5],
                device_id=(lax.rem(me + j, n), rep),
                device_id_type=pl.DeviceIdType.MESH,
            ).start()
            return 0

        lax.fori_loop(1, n, one, 0)
        pltpu.make_async_copy(parts.at[0], tile(whole, mine), recv_sem.at[5]).start()

    lax.fori_loop(0, EARLY // 2, backward_sending, 0)
    at = width
    for p in range(3):
        grads[at : at + early, :] = dg(
            qkv[p * width : p * width + early, :], norm[...], 1, 1
        ).astype(BF)
        at += early
    send_tiles(0, tiles)
    backward_plain(EARLY // 2, 0)
    pl.when(is_early)(sum_tile)
    backward_plain(EARLY // 2 + 1, 0)
    pl.when(is_early)(share_tile)
    lax.fori_loop(EARLY // 2 + 2, HEADS // 2, backward_plain, 0)
    for p in range(3):
        grads[at : at + late, :] = dg(
            qkv[p * width + early : (p + 1) * width, :], norm[...], 1, 1
        ).astype(BF)
        at += late
    send_tiles(tiles, n)

    d_norm = jnp.dot(w_qkv[...], qkv[...], preferred_element_type=F32)
    values = x16[...].astype(F32)
    center = jnp.mean(values, axis=0, keepdims=True)
    spread = jnp.mean(jnp.square(values - center), axis=0, keepdims=True)
    scale = lax.rsqrt(spread + 1e-05)
    unit = (values - center) * scale
    along = jnp.mean(d_norm * unit, axis=0, keepdims=True)
    level = jnp.mean(d_norm, axis=0, keepdims=True)
    d_rows = (c16[...].astype(F32) + scale * (d_norm - level - unit * along)).astype(BF)
    wait_sent(send_b, 1)
    to_chunks(dg(seat[...], d_rows, 1, 1), send_b)
    send_some(send_b, got_g, 3, 1, n)
    send_own(send_b, got_g, 3)

    pl.when(jnp.logical_not(is_early))(sum_tile)
    wait_got(got_r, 2)
    from_chunks(got_r)
    out_r[...] = jnp.dot(back[...], rows[...], preferred_element_type=F32).astype(BF)
    pl.when(jnp.logical_not(is_early))(share_tile)
    wait_got(got_g, 3)
    from_chunks(got_g)
    out_g[...] = jnp.dot(back[...], rows[...], preferred_element_type=F32).astype(BF)
    pltpu.make_async_copy(whole, whole, recv_sem.at[5]).wait()
    pieces = []
    for p in range(3):
        at = width + p * early
        pieces.append(whole[at : at + early, :])
        at = width + 3 * early + p * late
        pieces.append(whole[at : at + late, :])
    out_wq[...] = jnp.transpose(jnp.concatenate(pieces, axis=0).astype(F32))
    out_wo[...] = whole[:width, :].astype(F32)
    wait_sent(send_a, 2)
    wait_sent(send_b, 3)
    wait_sent(parts, 4)
    wait_sent(parts, 5)


def on_device(feats, cotangent, dest, pads, w_qkv, w_out):
    n = lax.axis_size("pts")
    points = feats.shape[1]
    width = feats.shape[2]
    factor = float((n * lax.axis_size("rep") * points) ** (-0.5))
    vmem = pl.BlockSpec(memory_space=pltpu.VMEM)
    got = pl.pallas_call(
        functools.partial(kernel, n, factor),
        out_shape=(
            jax.ShapeDtypeStruct((points, width), BF),
            jax.ShapeDtypeStruct((points, width), BF),
            jax.ShapeDtypeStruct((width, 3 * width), F32),
            jax.ShapeDtypeStruct((width, width), F32),
        ),
        in_specs=[vmem, vmem, vmem, pl.BlockSpec(memory_space=pltpu.SMEM), vmem, vmem],
        out_specs=(vmem, vmem, vmem, vmem),
        scratch_shapes=[
            pltpu.VMEM((points, CAP * n), BF),
            pltpu.VMEM((CAP * n, PATCH), BF),
            pltpu.VMEM((n * CHUNK, 128), F32),
            *[pltpu.VMEM((n, CHUNK, 128), BF)] * 6,
            pltpu.VMEM((CAP * n, width), BF),
            pltpu.VMEM((width, PATCH), BF),
            pltpu.VMEM((width, PATCH), BF),
            pltpu.VMEM((width, PATCH), BF),
            pltpu.VMEM((3 * width, PATCH), BF),
            pltpu.VMEM((width, PATCH), BF),
            pltpu.VMEM((width, PATCH), BF),
            pltpu.VMEM((width, PATCH), F32),
            pltpu.VMEM((HEADS, 1, PATCH), F32),
            pltpu.VMEM((HEADS, PATCH, PATCH), BF),
            pltpu.VMEM((4 * width, width), BF),
            pltpu.VMEM((n, 16, 128), BF),
            pltpu.VMEM((16, 128), F32),
            pltpu.VMEM((16, 128), F32),
            pltpu.VMEM((4 * width, width), BF),
            pltpu.SemaphoreType.DMA((6,)),
            pltpu.SemaphoreType.DMA((6,)),
            pltpu.SemaphoreType.DMA((2,)),
        ],
        compiler_params=pltpu.CompilerParams(
            collective_id=0, has_side_effects=True, vmem_limit_bytes=62 * 2**20
        ),
        cost_estimate=pl.CostEstimate(flops=4 * 10**9, bytes_accessed=4 * 10**6, transcendentals=17 * 10**6),
    )(feats[0], cotangent[0], dest, pads, w_qkv, w_out)
    return (got[0][None], got[1][None], got[2], got[3])


def solution(mesh):
    placed = (
        P("rep", "pts", None),
        P("rep", "pts", None),
        P("rep", "pts"),
        P("rep", "pts"),
        P(),
        P(),
    )
    return jax.shard_map(
        on_device,
        mesh=mesh,
        in_specs=placed,
        out_specs=(P("rep", "pts", None), P("rep", "pts", None), P(), P()),
        check_vma=False,
    )
```

time: 156 us -> 149 us (0.955)
  Pallas kernels: 150 us -> 143 us
    pallas_call x1, Pallas kernels: 150 us -> 143 us  [on_device(): pl.pallas_call(functools.partial(kernel, n, factor), out_shape=(jax.Shape...]
where the time goes in v2:
time: 149 us
  Pallas kernels  143 us (96%)
  local copies, waits for them, and re-layouts  4.41 us (3%)
    pallas_call x1, Pallas kernels, on_device(): pl.pallas_call(functools.partial(kernel, n, factor), out_shape=(jax.Shape...  143 us
    unnamed x10, local copies, waits for them, and re-layouts  4.41 us

profile of v2, /device:TPU:1, one launch (start us, length us, event | category | flops | bytes accessed | tf_op | source)
XLA Modules:
  0.0 148.5 jit_solution(16892870550301188690)
XLA Ops:
  1.3 142.8 %shard_map.93 = (bf16[768,256]{1,0:T(8,128)(2,1)}, bf16[768,256]{1,0:T(8,128)(2,1)}, f32[256,768]{1,0:T(8,128)}, f32[256,256]{1,0:T(8,128)}) custom-call(bf16[768,256]{1,0:T(8,128)(2,1)} %bitcast.6, bf16[768,256]{1,0:T(8,128)(2,1)} %bitcast.7, s32[1,768]{1,0:T(1,128)} %dest.1, s32[1,1]{1,0:T(1,128)S(6)} %copy.14.pads, bf16[256,768]{1,0:T(8,128)(2,1)} %w_qkv.1, ...), custom_call_target="tpu_custom_call" | custom-call | flops 4000000000 | bytes 4000000 | tf_op jit(solution)/shard_map/pallas_call | solution.py:371
  144.1 0.0 copy-start.1
  144.1 0.0 copy-start
  144.1 1.9 %copy.15 = bf16[1,768,256]{2,1,0:T(8,128)(2,1)} copy(bf16[1,768,256]{2,1,0:T(8,128)(2,1)} %bitcast.5) | data formatting | bytes 786432
  146.0 0.0 copy-done.1
  146.0 0.7 copy.16
  146.7 0.0 copy-done
  146.7 0.0 copy-start.2
  146.7 0.9 copy.17
  147.6 0.2 copy-done.2
  147.8 0.7 copy.18
Async XLA Ops:
  144.1 1.9 %copy-start.1 = (bf16[768,256]{1,0:T(8,128)(2,1)S(1)}, bf16[768,256]{1,0:T(8,128)(2,1)}, u32[]{:S(2)}) copy-start(bf16[768,256]{1,0:T(8,128)(2,1)} %get-tuple-element.9) | copy-start | bytes 1179652
  144.1 2.6 %copy-start = (f32[256,768]{1,0:T(8,128)S(1)}, f32[256,768]{1,0:T(8,128)}, u32[]{:S(2)}) copy-start(f32[256,768]{1,0:T(8,128)} %get-tuple-element.18) | copy-start | bytes 2359300
  146.7 1.1 copy-start.2

commit v3 on v2

--- a/solution.py
+++ b/solution.py
@@ -12,9 +12,11 @@
 PATCH = 1024
 CAP = 10
 CHUNK = 24
-EARLY = 10
-MIX = 45
-UNMIX = 37
+EARLY = 8
+RING = 8
+SIDE = 4
+PLANE = SIDE * SIDE
+MIX = 7
 BF = jnp.bfloat16
 F32 = jnp.float32
 
@@ -33,7 +35,7 @@
     out_r, out_g, out_wq, out_wo,
     back, seat, stage, send_a, send_b, got_f, got_c, got_r, got_g,
     rows, x16, c16, norm, qkv, att, d_att, o32, inv, expo,
-    grads, parts, total, other, whole,
+    grads, parts, plane_sum, strips, total, other, scaled, done, ready, whole,
     send_sem, recv_sem, pair_sem,
 ):
     me = lax.axis_index("pts")
@@ -189,7 +191,7 @@
     wait_sent(send_a, 0)
     to_chunks(dg(seat[...], out_t, 1, 1), send_a)
     wait_got(got_c, 1)
-    send_some(send_a, got_r, 2, 1, 3)
+    send_some(send_a, got_r, 2, 1, 4)
     send_own(send_a, got_r, 2)
     from_chunks(got_c)
     c16[...] = dg(rows[...], seat[...], 0, 0).astype(BF)
@@ -234,47 +236,66 @@
         pending()
 
     def backward_sending(step, _):
-        backward(step, 3, 25)
-        return 0
-
-    def backward_plain(step, _):
-        backward(step, 0, 0)
+        backward(step, 4, 31)
         return 0
 
     early = EARLY * CH
     late = width - early
-    tiles = (width + 3 * early) // 8
-    mine = lax.rem(me * UNMIX, n)
-    is_early = mine < tiles
-
-    def tile(ref, t):
-        return ref.at[
-            pl.ds(pl.multiple_of((t // 2) * 16, 16), 16), pl.ds(pl.multiple_of((t % 2) * 128, 128), 128)
-        ]
-
-    def send_tiles(lo, hi):
+    depth = 4 * width // PLANE
+    strip = depth // RING
+    split = (width + 3 * early) // depth
+    at_z = lax.rem(me // SIDE, RING)
+    member = (me // (SIDE * RING)) * SIDE + lax.rem(me, SIDE)
+    mine = lax.rem(member * MIX, PLANE)
+    is_early = mine < split
+
+    def in_plane(other_member):
+        return (other_member // SIDE) * (SIDE * RING) + at_z * SIDE + lax.rem(other_member, SIDE)
+
+    def block(ref, b):
+        return ref.at[pl.ds(pl.multiple_of(b * depth, depth), depth), :]
+
+    def strip_of(ref, z):
+        return ref.at[pl.ds(pl.multiple_of(z * strip, strip), strip), :]
+
+    def remote(src, dst, which, peer):
+        return pltpu.make_async_remote_copy(
+            src_ref=src, dst_ref=dst, send_sem=send_sem.at[which], recv_sem=recv_sem.at[which],
+            device_id=(peer, rep), device_id_type=pl.DeviceIdType.MESH,
+        )
+
+    def send_blocks(lo, hi):
         def one(j, _):
-            t = lo + lax.rem(j + me, hi - lo)
-            peer = lax.rem(t * MIX, n)
+            b = lo + lax.rem(j + member, hi - lo)
+            peer = in_plane(lax.rem(b * MIX, PLANE))
 
             @pl.when(peer != me)
             def _():
-                pltpu.make_async_remote_copy(
-                    src_ref=tile(grads, t),
-                    dst_ref=parts.at[me],
-                    send_sem=send_sem.at[4],
-                    recv_sem=recv_sem.at[4],
-                    device_id=(peer, rep),
-                    device_id_type=pl.DeviceIdType.MESH,
-                ).start()
+                remote(block(grads, b), parts.at[member], 4, peer).start()
 
             @pl.when(peer == me)
             def _():
-                pltpu.make_async_copy(tile(grads, mine), parts.at[me], recv_sem.at[4]).start()
+                pltpu.make_async_copy(block(grads, mine), parts.at[member], recv_sem.at[4]).start()
 
             return 0
 
         lax.fori_loop(0, hi - lo, one, 0)
+
+    def along_z(j):
+        z = lax.rem(at_z + j, RING)
+        return z, (me // (SIDE * RING)) * (SIDE * RING) + z * SIDE + lax.rem(me, SIDE)
+
+    def sum_block():
+        wait_got(parts, 4)
+        plane_sum[...] = jnp.sum(parts[...].astype(F32), axis=0)
+
+        def one(j, _):
+            z, peer = along_z(j)
+            remote(strip_of(plane_sum, z), strips.at[at_z], 6, peer).start()
+            return 0
+
+        lax.fori_loop(1, RING, one, 0)
+        pltpu.make_async_copy(strip_of(plane_sum, at_z), strips.at[at_z], recv_sem.at[6]).start()
 
     def swap():
         return pltpu.make_async_remote_copy(
@@ -282,28 +303,39 @@
             device_id=(me, 1 - rep), device_id_type=pl.DeviceIdType.MESH,
         )
 
-    def sum_tile():
-        wait_got(parts, 4)
-        total[...] = jnp.sum(parts[...].astype(F32), axis=0)
+    def swap_strip():
+        wait_got(strips, 6)
+        total[...] = jnp.sum(strips[...], axis=0)
         swap().start()
 
-    def share_tile():
+    def gather_strip():
         swap().wait()
-        parts[0] = ((total[...] + other[...]) * factor).astype(BF)
+        scaled[...] = (total[...] + other[...]) * factor
 
         def one(j, _):
-            pltpu.make_async_remote_copy(
-                src_ref=parts.at[0],
-                dst_ref=tile(whole, mine),
-                send_sem=send_sem.at[5],
-                recv_sem=recv_sem.at[5],
-                device_id=(lax.rem(me + j, n), rep),
-                device_id_type=pl.DeviceIdType.MESH,
-            ).start()
+            _, peer = along_z(j)
+            remote(scaled, strip_of(done, at_z), 7, peer).start()
             return 0
 
-        lax.fori_loop(1, n, one, 0)
-        pltpu.make_async_copy(parts.at[0], tile(whole, mine), recv_sem.at[5]).start()
+        lax.fori_loop(1, RING, one, 0)
+        pltpu.make_async_copy(scaled, strip_of(done, at_z), recv_sem.at[7]).start()
+
+    def share_block():
+        wait_got(done, 7)
+        ready[...] = done[...].astype(BF)
+
+        def one(j, _):
+            remote(ready, block(whole, mine), 5, in_plane(lax.rem(member + j, PLANE))).start()
+            return 0
+
+        lax.fori_loop(1, PLANE, one, 0)
+        pltpu.make_async_copy(ready, block(whole, mine), recv_sem.at[5]).start()
+
+    def backward_late(step, _):
+        backward(step, 0, 0)
+        for after, job in enumerate((sum_block, swap_strip, gather_strip, share_block)):
+            pl.when(is_early & (step == EARLY // 2 + after))(job)
+        return 0
 
     lax.fori_loop(0, EARLY // 2, backward_sending, 0)
     at = width
@@ -312,18 +344,14 @@
             qkv[p * width : p * width + early, :], norm[...], 1, 1
         ).astype(BF)
         at += early
-    send_tiles(0, tiles)
-    backward_plain(EARLY // 2, 0)
-    pl.when(is_early)(sum_tile)
-    backward_plain(EARLY // 2 + 1, 0)
-    pl.when(is_early)(share_tile)
-    lax.fori_loop(EARLY // 2 + 2, HEADS // 2, backward_plain, 0)
+    send_blocks(0, split)
+    lax.fori_loop(EARLY // 2, HEADS // 2, backward_late, 0)
     for p in range(3):
         grads[at : at + late, :] = dg(
             qkv[p * width + early : (p + 1) * width, :], norm[...], 1, 1
         ).astype(BF)
         at += late
-    send_tiles(tiles, n)
+    send_blocks(split, PLANE)
 
     d_norm = jnp.dot(w_qkv[...], qkv[...], preferred_element_type=F32)
     values = x16[...].astype(F32)
@@ -339,11 +367,14 @@
     send_some(send_b, got_g, 3, 1, n)
     send_own(send_b, got_g, 3)
 
-    pl.when(jnp.logical_not(is_early))(sum_tile)
+    is_late = jnp.logical_not(is_early)
+    pl.when(is_late)(sum_block)
     wait_got(got_r, 2)
     from_chunks(got_r)
+    pl.when(is_late)(swap_strip)
     out_r[...] = jnp.dot(back[...], rows[...], preferred_element_type=F32).astype(BF)
-    pl.when(jnp.logical_not(is_early))(share_tile)
+    pl.when(is_late)(gather_strip)
+    pl.when(is_late)(share_block)
     wait_got(got_g, 3)
     from_chunks(got_g)
     out_g[...] = jnp.dot(back[...], rows[...], preferred_element_type=F32).astype(BF)
@@ -358,14 +389,16 @@
     out_wo[...] = whole[:width, :].astype(F32)
     wait_sent(send_a, 2)
     wait_sent(send_b, 3)
-    wait_sent(parts, 4)
-    wait_sent(parts, 5)
+    for which, ref, copies in ((4, parts, PLANE - 1), (5, parts, PLANE - 1), (6, strips, RING - 1), (7, strips, RING - 1)):
+        part = ref.at[pl.ds(0, copies)]
+        pltpu.make_async_copy(part, part, send_sem.at[which]).wait()
 
 
 def on_device(feats, cotangent, dest, pads, w_qkv, w_out):
     n = lax.axis_size("pts")
     points = feats.shape[1]
     width = feats.shape[2]
+    depth = 4 * width // PLANE
     factor = float((n * lax.axis_size("rep") * points) ** (-0.5))
     vmem = pl.BlockSpec(memory_space=pltpu.VMEM)
     got = pl.pallas_call(
@@ -394,12 +427,17 @@
             pltpu.VMEM((HEADS, 1, PATCH), F32),
             pltpu.VMEM((HEADS, PATCH, PATCH), BF),
             pltpu.VMEM((4 * width, width), BF),
-            pltpu.VMEM((n, 16, 128), BF),
-            pltpu.VMEM((16, 128), F32),
-            pltpu.VMEM((16, 128), F32),
+            pltpu.VMEM((PLANE, depth, width), BF),
+            pltpu.VMEM((depth, width), F32),
+            pltpu.VMEM((RING, depth // RING, width), F32),
+            pltpu.VMEM((depth // RING, width), F32),
+            pltpu.VMEM((depth // RING, width), F32),
+            pltpu.VMEM((depth // RING, width), F32),
+            pltpu.VMEM((depth, width), F32),
+            pltpu.VMEM((depth, width), BF),
             pltpu.VMEM((4 * width, width), BF),
-            pltpu.SemaphoreType.DMA((6,)),
-            pltpu.SemaphoreType.DMA((6,)),
+            pltpu.SemaphoreType.DMA((8,)),
+            pltpu.SemaphoreType.DMA((8,)),
             pltpu.SemaphoreType.DMA((2,)),
         ],
         compiler_params=pltpu.CompilerParams(

time: 149 us -> 149 us (level); the launches traced: 149 us -> 147 us
  Pallas kernels: 143 us -> 141 us
    pallas_call x1, Pallas kernels: 143 us -> 141 us  [on_device(): pl.pallas_call(functools.partial(kernel, n, factor), out_shape=(jax.Shape...]
where the time goes in v3:
time: 149 us; the launch traced here: 147 us
  Pallas kernels  141 us (95%)
  local copies, waits for them, and re-layouts  4.41 us (3%)
    pallas_call x1, Pallas kernels, on_device(): pl.pallas_call(functools.partial(kernel, n, factor), out_shape=(jax.Shape...  141 us
    unnamed x10, local copies, waits for them, and re-layouts  4.41 us

profile of v3, /device:TPU:1, one launch (start us, length us, event | category | flops | bytes accessed | tf_op | source)
XLA Modules:
  0.0 147.0 jit_solution(2597209225962384201)
XLA Ops:
  1.3 141.2 %shard_map.93 = (bf16[768,256]{1,0:T(8,128)(2,1)}, bf16[768,256]{1,0:T(8,128)(2,1)}, f32[256,768]{1,0:T(8,128)}, f32[256,256]{1,0:T(8,128)}) custom-call(bf16[768,256]{1,0:T(8,128)(2,1)} %bitcast.6, bf16[768,256]{1,0:T(8,128)(2,1)} %bitcast.7, s32[1,768]{1,0:T(1,128)} %dest.1, s32[1,1]{1,0:T(1,128)S(6)} %copy.14.pads, bf16[256,768]{1,0:T(8,128)(2,1)} %w_qkv.1, ...), custom_call_target="tpu_custom_call" | custom-call | flops 4000000000 | bytes 4000000 | tf_op jit(solution)/shard_map/pallas_call | solution.py:404
  142.5 0.0 copy-start.1
  142.5 0.0 copy-start
  142.5 1.9 %copy.15 = bf16[1,768,256]{2,1,0:T(8,128)(2,1)} copy(bf16[1,768,256]{2,1,0:T(8,128)(2,1)} %bitcast.5) | data formatting | bytes 786432
  144.4 0.0 copy-done.1
  144.4 0.7 copy.16
  145.2 0.0 copy-done
  145.2 0.0 copy-start.2
  145.2 0.9 copy.17
  146.0 0.2 copy-done.2
  146.2 0.7 copy.18
Async XLA Ops:
  142.5 1.9 %copy-start.1 = (bf16[768,256]{1,0:T(8,128)(2,1)S(1)}, bf16[768,256]{1,0:T(8,128)(2,1)}, u32[]{:S(2)}) copy-start(bf16[768,256]{1,0:T(8,128)(2,1)} %get-tuple-element.9) | copy-start | bytes 1179652
  142.5 2.6 %copy-start = (f32[256,768]{1,0:T(8,128)S(1)}, f32[256,768]{1,0:T(8,128)}, u32[]{:S(2)}) copy-start(f32[256,768]{1,0:T(8,128)} %get-tuple-element.18) | copy-start | bytes 2359300
  145.2 1.1 copy-start.2

commit v4 on v3

--- a/solution.py
+++ b/solution.py
@@ -333,8 +333,8 @@
 
     def backward_late(step, _):
         backward(step, 0, 0)
-        for after, job in enumerate((sum_block, swap_strip, gather_strip, share_block)):
-            pl.when(is_early & (step == EARLY // 2 + after))(job)
+        for after, job in enumerate((sum_block, swap_strip, gather_strip)):
+            pl.when(is_early & (step == EARLY // 2 + 1 + after))(job)
         return 0
 
     lax.fori_loop(0, EARLY // 2, backward_sending, 0)
@@ -368,6 +368,7 @@
     send_own(send_b, got_g, 3)
 
     is_late = jnp.logical_not(is_early)
+    pl.when(is_early)(share_block)
     pl.when(is_late)(sum_block)
     wait_got(got_r, 2)
     from_chunks(got_r)

time: 149 us -> 145 us (0.973)
  Pallas kernels: 141 us -> 138 us
    pallas_call x1, Pallas kernels: 141 us -> 138 us  [on_device(): pl.pallas_call(functools.partial(kernel, n, factor), out_shape=(jax.Shape...]
where the time goes in v4:
time: 145 us; the launch traced here: 144 us
  Pallas kernels  138 us (95%)
  local copies, waits for them, and re-layouts  4.41 us (3%)
    pallas_call x1, Pallas kernels, on_device(): pl.pallas_call(functools.partial(kernel, n, factor), out_shape=(jax.Shape...  138 us
    unnamed x10, local copies, waits for them, and re-layouts  4.41 us

profile of v4, /device:TPU:1, one launch (start us, length us, event | category | flops | bytes accessed | tf_op | source)
XLA Modules:
  0.0 143.8 jit_solution(5374900840073237255)
XLA Ops:
  1.3 138.1 %shard_map.93 = (bf16[768,256]{1,0:T(8,128)(2,1)}, bf16[768,256]{1,0:T(8,128)(2,1)}, f32[256,768]{1,0:T(8,128)}, f32[256,256]{1,0:T(8,128)}) custom-call(bf16[768,256]{1,0:T(8,128)(2,1)} %bitcast.6, bf16[768,256]{1,0:T(8,128)(2,1)} %bitcast.7, s32[1,768]{1,0:T(1,128)} %dest.1, s32[1,1]{1,0:T(1,128)S(6)} %copy.14.pads, bf16[256,768]{1,0:T(8,128)(2,1)} %w_qkv.1, ...), custom_call_target="tpu_custom_call" | custom-call | flops 4000000000 | bytes 4000000 | tf_op jit(solution)/shard_map/pallas_call | solution.py:405
  139.4 0.0 copy-start.1
  139.4 0.0 copy-start
  139.4 1.9 %copy.15 = bf16[1,768,256]{2,1,0:T(8,128)(2,1)} copy(bf16[1,768,256]{2,1,0:T(8,128)(2,1)} %bitcast.5) | data formatting | bytes 786432
  141.3 0.0 copy-done.1
  141.3 0.7 copy.16
  142.0 0.0 copy-done
  142.0 0.0 copy-start.2
  142.1 0.9 copy.17
  142.9 0.2 copy-done.2
  143.1 0.7 copy.18
Async XLA Ops:
  139.4 1.9 %copy-start.1 = (bf16[768,256]{1,0:T(8,128)(2,1)S(1)}, bf16[768,256]{1,0:T(8,128)(2,1)}, u32[]{:S(2)}) copy-start(bf16[768,256]{1,0:T(8,128)(2,1)} %get-tuple-element.9) | copy-start | bytes 1179652
  139.4 2.6 %copy-start = (f32[256,768]{1,0:T(8,128)S(1)}, f32[256,768]{1,0:T(8,128)}, u32[]{:S(2)}) copy-start(f32[256,768]{1,0:T(8,128)} %get-tuple-element.18) | copy-start | bytes 2359300
  142.0 1.1 copy-start.2
